TPU v7x, 512 devices: a whole 4x4x16 slice. The times are simulated.
512 devices in a mesh: user: 16 (over x_lo, y, core), item: 32 (over z, x_hi).
Axes of the slice: x: 4 (x_hi: 2, x_lo: 2; x = x_hi * 2 + x_lo), y: 4, z: 16, core: 2. Of those that a mesh axis runs over, the one named last changes fastest.
Arguments:
- user_emb: float32 [24576, 128], P(('user', 'item')), may hold values from -6 to 6
- item_emb: float32 [65536, 128], P(('item', 'user')), may hold values from -6 to 6
- user_deg: int32 [24576], P('user'), may hold values from 1 to 8
- item_deg: int32 [65536], P('item'), may hold values from 1 to 8
- tile_rows: int32 [16, 32, 128], P('user', 'item'), may hold values from 0 to 11
- tile_cols: int32 [16, 32, 128], P('user', 'item'), may hold values from 0 to 15
- tile_count: int32 [16, 32], P('user', 'item'), may hold values from 1 to 128, as said below
- tiles: bfloat16 [16, 32, 128, 128, 128], P('user', 'item'), may hold values from -0.125 to 0.125
Outputs:
- user_out: float32 [24576, 128], P(('user', 'item'))
- item_out: float32 [65536, 128], P(('item', 'user'))
Inputs may be any that keep to these rules, and one draw needn't show every extreme that they name: `tile_count`: every device has at least one live slot; on some device all 128 slots are live.
All inputs are finite; a program needn't handle non-finite values.
Results may differ from a plain program's by a relative error of at most 0.0029.
Values may be sent and summed in bfloat16 or wider, within the bound.
A program may use at most 64 MiB of HBM per device.

v0:
```python
import jax
import jax.numpy as jnp
from jax import lax
from jax.sharding import PartitionSpec as P


def fetch_items(item_src):
    return lax.all_gather(item_src, "user", axis=0, tiled=True)


def fetch_users(user_src):
    return lax.all_gather(user_src, "item", axis=0, tiled=True)


def reduce_users(user_total, feature):
    return lax.psum_scatter(
        user_total.reshape(-1, feature), "item", scatter_dimension=0, tiled=True
    )


def reduce_items(item_total, feature):
    return lax.psum_scatter(
        item_total.reshape(-1, feature), "user", scatter_dimension=0, tiled=True
    )


def local(user_emb, item_emb, user_deg, item_deg, tile_rows, tile_cols, tile_count, tiles):
    tile_side = tiles.shape[-1]
    feature = user_emb.shape[1]
    slot_total = tiles.shape[2]
    slab_tiles = tiles.reshape(slot_total, tile_side, tile_side)
    row_ids = tile_rows.reshape(slot_total)
    col_ids = tile_cols.reshape(slot_total)
    live_count = tile_count.reshape(())
    user_nblocks = user_deg.shape[0] // tile_side
    item_nblocks = item_deg.shape[0] // tile_side
    my_user = lax.axis_index("user")
    my_item = lax.axis_index("item")
    user_scale_all = lax.rsqrt(user_deg.astype(jnp.float32))
    item_scale_all = lax.rsqrt(item_deg.astype(jnp.float32))
    own_user_scale = lax.dynamic_slice_in_dim(
        user_scale_all, my_item * user_emb.shape[0], user_emb.shape[0], 0
    )
    own_item_scale = lax.dynamic_slice_in_dim(
        item_scale_all, my_user * item_emb.shape[0], item_emb.shape[0], 0
    )
    user_src = (user_emb * own_user_scale[:, None]).astype(jnp.bfloat16)
    item_src = (item_emb * own_item_scale[:, None]).astype(jnp.bfloat16)
    group_size = min(16, slot_total)
    turn_count = slot_total // group_size

    def sweep(item_blocks, user_blocks):

        def advance(turn_index, state_pair):
            user_total, item_total = state_pair
            first_slot = turn_index * group_size
            tile_group = lax.dynamic_slice_in_dim(slab_tiles, first_slot, group_size, 0)
            rows_now = lax.dynamic_slice_in_dim(row_ids, first_slot, group_size, 0)
            cols_now = lax.dynamic_slice_in_dim(col_ids, first_slot, group_size, 0)
            slot_now = first_slot + jnp.arange(group_size, dtype=jnp.int32)
            alive_mask = (slot_now < live_count).astype(jnp.float32)
            if item_blocks is not None:
                chosen = item_blocks[cols_now]
                product = jnp.einsum(
                    "tij,tjd->tid", tile_group, chosen, preferred_element_type=jnp.float32
                )
                user_total = user_total.at[rows_now].add(product * alive_mask[:, None, None])
            if user_blocks is not None:
                chosen = user_blocks[rows_now]
                product = jnp.einsum(
                    "tji,tjd->tid", tile_group, chosen, preferred_element_type=jnp.float32
                )
                item_total = item_total.at[cols_now].add(product * alive_mask[:, None, None])
            return (user_total, item_total)

        start_pair = (
            jnp.zeros((user_nblocks, tile_side, feature), jnp.float32),
            jnp.zeros((item_nblocks, tile_side, feature), jnp.float32),
        )
        return lax.fori_loop(0, turn_count, advance, start_pair)

    item_column = fetch_items(item_src).reshape(item_nblocks, tile_side, feature)
    user_total, unused_items = sweep(item_column, None)
    user_sum = reduce_users(user_total, feature)
    user_row = fetch_users(user_src).reshape(user_nblocks, tile_side, feature)
    unused_users, item_total = sweep(None, user_row)
    item_sum = reduce_items(item_total, feature)
    user_out = user_sum * own_user_scale[:, None]
    item_out = item_sum * own_item_scale[:, None]
    return (user_out, item_out)


def solution(mesh):
    return jax.shard_map(
        local,
        mesh=mesh,
        in_specs=(
            P(("user", "item"), None),
            P(("item", "user"), None),
            P("user"),
            P("item"),
            P("user", "item", None),
            P("user", "item", None),
            P("user", "item"),
            P("user", "item", None, None, None),
        ),
        out_specs=(P(("user", "item"), None), P(("item", "user"), None)),
        check_vma=False,
    )
```

profile of v0, /device:TPU:1, one launch (start us, length us, event | category | flops | bytes accessed | tf_op | source)
XLA Modules:
  0.0 913.8 jit_solution(8064739614643571868)
XLA Ops:
  7.2 0.8 fusion.4
  8.0 0.8 multiply_convert_fusion.1
  8.8 71.5 %all_gather.7 = bf16[1536,128]{1,0:T(8,128)(2,1)S(1)} all-gather(bf16[48,128]{1,0:T(8,128)(2,1)S(1)} %multiply_convert_fusion.1), channel_id=1, replica_groups=mesh['user'=16,'item'=32] {'item'}, dimensions={0}, use_global_device_ids=true | all-gather | bytes 405504 | tf_op jit(solution)/shard_map/all_gather | solution.py:12
  80.3 6.4 copy.10
  86.8 35.2 %while.27 = (s32[]{:T(128)}, f32[16,128,128]{2,1,0:T(8,128)S(1)}, s32[128]{0:T(128)S(1)}, bf16[128,128,128]{1,2,0:T(8,128)(2,1)}, s32[128]{0:T(128)S(1)}, /*inde...) while((s32[]{:T(128)}, f32[16,128,128]{2,1,0:T(8,128)S(1)}, ...), condition=%wide.region_6.0_spmd, body=%wide.region_4.0_spmd.sunk | while | flops 67634328 | bytes 6296299 | solution.py:80
  88.2 1.4 convolution_multiply_fusion.5
  89.6 1.6 scatter_fusion.1
  92.6 1.4 convolution_multiply_fusion.5
  94.0 1.6 scatter_fusion.1
  96.3 0.7 compare_convert_fusion.5
  97.0 1.4 convolution_multiply_fusion.5
  98.4 1.6 scatter_fusion.1
  101.4 1.4 convolution_multiply_fusion.5
  102.8 1.6 scatter_fusion.1
  105.8 1.4 convolution_multiply_fusion.5
  107.2 1.6 scatter_fusion.1
  109.5 0.7 compare_convert_fusion.5
  110.2 1.4 convolution_multiply_fusion.5
  111.5 1.6 scatter_fusion.1
  114.6 1.4 convolution_multiply_fusion.5
  115.9 1.6 scatter_fusion.1
  119.0 1.4 convolution_multiply_fusion.5
  120.3 1.6 scatter_fusion.1
  122.0 1.0 copy-done.1
  123.0 0.8 fusion.5
  123.8 73.6 %reduce-scatter.5.cloned.1.call-done = f32[128,128]{1,0:T(8,128)} async-done(((f32[2048,128]{1,0:T(8,128)}), f32[128,128]{1,0:T(8,128)}) %reduce-scatter.5.cloned.1.call-update) | async-done | bytes 65552 | tf_op jit(solution)/shard_map/reduce_scatter | solution.py:22
  197.4 1.6 broadcast_multiply_fusion
  199.0 20.7 %all_gather.6 = bf16[2048,128]{1,0:T(8,128)(2,1)S(1)} all-gather(bf16[128,128]{1,0:T(8,128)(2,1)S(1)} %get-tuple-element.292), channel_id=1, replica_groups=mesh['user'=16,'item'=32] {'user'}, dimensions={0}, use_global_device_ids=true | all-gather | bytes 557056 | tf_op jit(solution)/shard_map/all_gather | solution.py:8
  219.7 35.2 %while.26 = (s32[]{:T(128)}, f32[12,128,128]{2,1,0:T(8,128)S(1)}, s32[128]{0:T(128)S(1)}, bf16[128,128,128]{2,1,0:T(8,128)(2,1)}, s32[128]{0:T(128)S(1)}, /*inde...) while((s32[]{:T(128)}, f32[12,128,128]{2,1,0:T(8,128)S(1)}, ...), condition=%wide.region_2.0_spmd, body=%wide.region_0.0_spmd.sunk | while | flops 67634328 | bytes 6296299 | solution.py:80
  221.1 1.4 convolution_multiply_fusion.4
  222.5 1.6 scatter_fusion
  225.5 1.4 convolution_multiply_fusion.4
  226.9 1.6 scatter_fusion
  229.9 1.4 convolution_multiply_fusion.4
  231.3 1.6 scatter_fusion
  234.3 1.4 convolution_multiply_fusion.4
  235.6 1.6 scatter_fusion
  238.7 1.4 convolution_multiply_fusion.4
  240.0 1.6 scatter_fusion
  243.1 1.4 convolution_multiply_fusion.4
  244.4 1.6 scatter_fusion
  247.5 1.4 convolution_multiply_fusion.4
  248.8 1.6 scatter_fusion
  251.9 1.4 convolution_multiply_fusion.4
  253.2 1.6 scatter_fusion
  254.9 0.9 copy-done
  255.8 649.8 %reduce-scatter.3.cloned.1.call-done = f32[48,128]{1,0:T(8,128)} async-done(((f32[1536,128]{1,0:T(8,128)}), f32[48,128]{1,0:T(8,128)}) %reduce-scatter.3.cloned.1.call-update) | async-done | bytes 24592 | tf_op jit(solution)/shard_map/reduce_scatter | solution.py:16
  905.6 1.4 broadcast_multiply_fusion.1
  (76 shorter events, 21.1 us)
Async XLA Ops:
  7.2 190.2 %reduce-scatter.5.cloned.1.call-start = ((), (), s32[]{:S(2)}) async-start(), calls=%async_computation.3 | async-start | bytes 1114112 | tf_op jit(solution)/shard_map/reduce_scatter | solution.py:22
  80.3 6.5 copy-start.3
  80.3 6.5 copy-start.4
  86.8 110.6 %copy-start.2 = (f32[128,128]{1,0:T(8,128)S(1)}, f32[128,128]{1,0:T(8,128)}, u32[]{:S(2)}) copy-start(f32[128,128]{1,0:T(8,128)} %param.13) | copy-start | bytes 196612
  122.0 1.0 copy-start.1
  123.0 782.6 %reduce-scatter.3.cloned.1.call-start = ((), (), s32[]{:S(2)}) async-start(), calls=%async_computation.2 | async-start | bytes 811008 | tf_op jit(solution)/shard_map/reduce_scatter | solution.py:16
  254.8 0.9 copy-start
Sparse Core Ops, SparseCore 0:
  123.1 74.2 reduce-scatter.4
  255.9 649.6 reduce-scatter.2
where the time goes:
time: 926 us; the launch traced here: 914 us
  waiting for transfers between devices  723 us (78%)
  blocking collectives  92.1 us (10%)
  other arithmetic  42.8 us (5%)
  matrix products  21.6 us (2%)
  local copies, waits for them, and re-layouts  18.8 us (2%)
  between operations  14.1 us (2%)
    reduce_scatter x1, waiting for transfers between devices, reduce_users(): lax.psum_scatter(user_total.reshape(-1, feature), 'item', scatter_dimensi...  650 us
    reduce_scatter x1, waiting for transfers between devices, reduce_items(): lax.psum_scatter(item_total.reshape(-1, feature), 'user', scatter_dimensi...  73.6 us
    all_gather x1, blocking collectives, fetch_users(): return lax.all_gather(user_src, 'item', axis=0, tiled=True)  71.5 us
    all_gather x1, blocking collectives, fetch_items(): return lax.all_gather(item_src, 'user', axis=0, tiled=True)  20.7 us
  transfers between devices with their start and end apart: 2, of which 2 were waited for; matrix products, arithmetic and copies ran while one was open for 0% of the time, Pallas kernels for 0%

commit v1 on v0

v1 whole, which is shorter than its diff:
```python
import functools

import jax
import jax.numpy as jnp
from jax import lax
from jax.experimental import pallas as pl
from jax.experimental.pallas import tpu as pltpu
from jax.sharding import PartitionSpec as P

MESH = pl.DeviceIdType.MESH
F32, BF16, I32 = jnp.float32, jnp.bfloat16, jnp.int32

USERS_AXIS = 16
BLOCK = 128
SLOTS = 128
UBLOCKS, IBLOCKS = 12, 16
SHARD = 48
UPAIRS = (SLOTS + UBLOCKS) // 2
IPAIRS = (SLOTS + IBLOCKS) // 2
LANES = 256


def iota(shape, dim):
    return lax.broadcasted_iota(I32, shape, dim)


def count(mask, dim):
    return jnp.sum(jnp.where(mask, 1, 0).astype(I32), axis=dim, keepdims=True)


def column(lanes):
    eye = iota((SLOTS, SLOTS), 0) == iota((SLOTS, SLOTS), 1)
    return jnp.sum(jnp.where(eye, lanes, 0), axis=1, keepdims=True)


def order(keys, others, live):
    keys_c, others_c = column(keys), column(others)
    at_lane, at_row = iota((SLOTS, SLOTS), 1), iota((SLOTS, SLOTS), 0)
    alive_l = at_lane < live
    alive_c = iota((SLOTS, 1), 0) < live
    ahead = (keys_c == keys) & (at_lane < at_row) & alive_l
    rank_c = count(ahead, 1)
    hits_l = count((keys_c == at_lane) & (at_row < live), 0)
    hits_c = column(hits_l)
    padded_l = ((hits_l + 1) >> 1) << 1
    padded_c = ((hits_c + 1) >> 1) << 1
    base_l = jnp.sum(jnp.where(at_row < at_lane, padded_c, 0), axis=0, keepdims=True)
    base_c = jnp.sum(jnp.where(at_lane < at_row, padded_l, 0), axis=1, keepdims=True)
    place_c = jnp.sum(jnp.where(at_lane < keys_c, padded_l, 0), axis=1, keepdims=True) + rank_c
    places = iota((SLOTS, LANES), 1)
    slots = iota((SLOTS, LANES), 0)
    mine = (place_c == places) & alive_c
    slot = jnp.sum(jnp.where(mine, slots + 1, 0), axis=0, keepdims=True)
    slot = jnp.where(slot == 0, SLOTS, slot - 1)
    other = jnp.sum(jnp.where(mine, others_c, 0), axis=0, keepdims=True)
    opens = (base_c == places) & (hits_c > 0)
    keep = 1 - jnp.minimum(count(opens, 0), 1)
    last = ((base_l + padded_l) >> 1) - 1
    last = jnp.maximum(last, 0)
    some = jnp.minimum(hits_l, 1)
    return slot, other, keep, last, some


def own_scale(deg_ref, first, rows):
    blocks = deg_ref.shape[0]
    out = jnp.zeros((rows, 1), I32)
    for b in range(blocks):
        here = iota((rows, BLOCK), 1) + b * BLOCK == iota((rows, BLOCK), 0) + first
        out = out + jnp.sum(jnp.where(here, deg_ref[b : b + 1, :], 0), axis=1, keepdims=True)
    return lax.rsqrt(out.astype(F32))


def layer(
    user_emb, item_emb, user_deg, item_deg, rows_ref, cols_ref, live_ref, tiles_hbm,
    user_out, item_out,
    tiles, item_src, users, user_src_t, meta_v, meta, run_u, run_i, part_u, part_i,
    got1, send2, got2, got_i,
    local_sem, ag_i_s, ag_i_r, ag_a_s, ag_a_r, ag_b_s, ag_b_r, rs1_s, rs1_r, rs2_s, rs2_r, rsi_s, rsi_r,
):
    u, i = lax.axis_index("user"), lax.axis_index("item")
    z, xh = i // 2, lax.rem(i, 2)
    zh, zl = z // 4, lax.rem(z, 4)
    kind = 2 * zl + xh

    def at(dz, other):
        half = 1 - xh if other else xh
        return {"item": 2 * lax.rem(z + dz + 16, 16) + half}

    load = pltpu.make_async_copy(tiles_hbm.at[0, 0], tiles.at[pl.ds(0, SLOTS)], local_sem.at[0])
    load.start()

    barrier = pltpu.get_barrier_semaphore()
    for k in range(1, 16):
        pl.semaphore_signal(barrier, inc=1, device_id={"user": lax.rem(u + k, 16)}, device_id_type=MESH)
    near = [(dz, o) for dz in (-2, -1, 0, 1, 2) for o in (False, True) if dz or o]
    far = [(4, False), (8, False), (12, False)]
    for dz, o in near + far:
        pl.semaphore_signal(barrier, inc=1, device_id=at(dz, o), device_id_type=MESH)

    scale_u = own_scale(user_deg, i * SHARD, SHARD)
    scale_i = own_scale(item_deg, u * BLOCK, BLOCK)
    item_src[u] = (item_emb[...] * scale_i).astype(BF16)
    users[zh, kind] = (user_emb[...] * scale_u).astype(BF16)
    pl.semaphore_wait(barrier, 15 + len(near) + len(far))

    ag_a, ag_i = [], []
    for k in range(1, 4):
        ag_a.append(pltpu.make_async_remote_copy(
            src_ref=users.at[zh, kind], dst_ref=users.at[zh, kind], send_sem=ag_a_s.at[k], recv_sem=ag_a_r.at[k],
            device_id=at(4 * k, False), device_id_type=MESH))
    for c in ag_a:
        c.start()
    for k in range(1, 16):
        ag_i.append(pltpu.make_async_remote_copy(
            src_ref=item_src.at[u], dst_ref=item_src.at[u], send_sem=ag_i_s.at[k], recv_sem=ag_i_r.at[k],
            device_id={"user": lax.rem(u + k, 16)}, device_id_type=MESH))
    for c in ag_i:
        c.start()

    rows, cols, live = rows_ref[0], cols_ref[0], live_ref[0, 0]
    parts = order(rows, cols, live) + order(cols, rows, live)
    meta_v[...] = jnp.zeros_like(meta_v)
    for n, part in enumerate(parts):
        meta_v[n : n + 1, 0 : part.shape[1]] = part
    to_scalar = pltpu.make_async_copy(meta_v, meta, local_sem.at[1])
    to_scalar.start()
    tiles[SLOTS] = jnp.zeros((BLOCK, BLOCK), BF16)
    to_scalar.wait()

    for c in ag_a:
        c.wait_recv()
    near_b = [(0, True), (1, False), (1, True), (-1, False), (-1, True)]
    ag_b = []

    def hop2(up):
        return 2 * lax.rem(z + 16 + jnp.where(up, 2, -2), 16)

    for n, (dz, o) in enumerate(near_b):
        ag_b.append(pltpu.make_async_remote_copy(
            src_ref=users.at[:, kind], dst_ref=users.at[:, kind], send_sem=ag_b_s.at[n], recv_sem=ag_b_r.at[n],
            device_id=at(dz, o), device_id_type=MESH))
    for half in range(2):
        ag_b.append(pltpu.make_async_remote_copy(
            src_ref=users.at[:, kind], dst_ref=users.at[:, kind], send_sem=ag_b_s.at[5 + half],
            recv_sem=ag_b_r.at[5 + xh], device_id={"item": hop2(xh == 0) + half}, device_id_type=MESH))
    for c in ag_b:
        c.start()

    load.wait()
    for c in ag_i:
        c.wait_recv()

    def user_step(q, acc):
        s0, s1 = meta[0, 2 * q], meta[0, 2 * q + 1]
        c0, c1 = meta[1, 2 * q], meta[1, 2 * q + 1]
        keep = meta[2, 2 * q].astype(F32)
        left = jnp.concatenate([tiles[s0], tiles[s1]], axis=1)
        right = jnp.concatenate([item_src[c0], item_src[c1]], axis=0)
        acc = acc * keep + jnp.dot(left, right, preferred_element_type=F32)
        run_u[q] = acc
        return acc

    lax.fori_loop(0, UPAIRS, user_step, jnp.zeros((BLOCK, BLOCK), F32), unroll=2)
    for r in range(UBLOCKS):
        total = (run_u[meta[3, r]] * meta[4, r].astype(F32)).astype(BF16)
        for j in range(8):
            g = 8 * r + j
            part_u[g // 24, (g % 24) // 3, 16 * (g % 3) : 16 * (g % 3) + 16, :] = total[16 * j : 16 * j + 16]

    rs1 = []
    for n, (dz, o) in enumerate(near_b):
        half = 1 - xh if o else xh
        there = 2 * lax.rem(zl + dz + 4, 4) + half
        rs1.append(pltpu.make_async_remote_copy(
            src_ref=part_u.at[:, there], dst_ref=got1.at[n], send_sem=rs1_s.at[n], recv_sem=rs1_r.at[n],
            device_id=at(dz, o), device_id_type=MESH))
    for half in range(2):
        there = 2 * lax.rem(zl + 2, 4) + half
        rs1.append(pltpu.make_async_remote_copy(
            src_ref=part_u.at[:, there], dst_ref=got1.at[5 + xh], send_sem=rs1_s.at[5 + half],
            recv_sem=rs1_r.at[5 + xh], device_id={"item": hop2(half == 0) + half}, device_id_type=MESH))
    for c in rs1:
        c.start()

    for n in range(5):
        ag_b[n].wait_recv()
    for half in range(2):
        pltpu.make_async_remote_copy(
            src_ref=users.at[:, kind], dst_ref=users.at[:, 2 * lax.rem(zl + 2, 4) + half], send_sem=ag_b_s.at[5 + half],
            recv_sem=ag_b_r.at[5 + half], device_id=at(1, False), device_id_type=MESH).wait_recv()
    for r in range(UBLOCKS):
        groups = []
        for j in range(8):
            g = 8 * r + j
            groups.append(users[g // 24, (g % 24) // 3, 16 * (g % 3) : 16 * (g % 3) + 16, :])
        user_src_t[r] = jnp.concatenate(groups, axis=0).T

    def item_step(q, acc):
        s0, s1 = meta[5, 2 * q], meta[5, 2 * q + 1]
        r0, r1 = meta[6, 2 * q], meta[6, 2 * q + 1]
        keep = meta[7, 2 * q].astype(F32)
        left = jnp.concatenate([user_src_t[r0], user_src_t[r1]], axis=1)
        right = jnp.concatenate([tiles[s0], tiles[s1]], axis=0)
        acc = acc * keep + jnp.dot(left, right, preferred_element_type=F32)
        run_i[q] = acc
        return acc

    lax.fori_loop(0, IPAIRS, item_step, jnp.zeros((BLOCK, BLOCK), F32), unroll=2)
    for c in range(IBLOCKS):
        part_i[c] = (run_i[meta[8, c]] * meta[9, c].astype(F32)).astype(BF16)
    rsi = []
    for k in range(1, 16):
        there = lax.rem(u + k, 16)
        rsi.append(pltpu.make_async_remote_copy(
            src_ref=part_i.at[there], dst_ref=got_i.at[k], send_sem=rsi_s.at[k], recv_sem=rsi_r.at[k],
            device_id={"user": there}, device_id_type=MESH))
    for c in rsi:
        c.start()

    for n in range(5):
        rs1[n].wait_recv()
    for half in range(2):
        pltpu.make_async_remote_copy(
            src_ref=part_u.at[:, kind], dst_ref=got1.at[5 + half], send_sem=rs1_s.at[5 + half],
            recv_sem=rs1_r.at[5 + half], device_id=at(1, False), device_id_type=MESH).wait_recv()
    for h in range(4):
        total = part_u[h, kind].astype(F32)
        for n in range(7):
            total = total + got1[n, h].astype(F32)
        send2[h] = total
        got2[0, h] = total.astype(BF16)
    rs2 = []
    for k in range(1, 4):
        there = lax.rem(zh + k, 4)
        rs2.append(pltpu.make_async_remote_copy(
            src_ref=got2.at[0, there], dst_ref=got2.at[k, 0], send_sem=rs2_s.at[k], recv_sem=rs2_r.at[k],
            device_id=at(4 * k, False), device_id_type=MESH))
    for c in rs2:
        c.start()

    for c in rsi:
        c.wait_recv()
    total = part_i[u].astype(F32)
    for k in range(1, 16):
        total = total + got_i[k].astype(F32)
    item_out[...] = total.T * scale_i

    for c in rs2:
        c.wait_recv()
    total = send2[zh]
    for k in range(1, 4):
        total = total + got2[k, 0].astype(F32)
    user_out[...] = total * scale_u

    for c in ag_a + ag_i + ag_b + rs1 + rs2 + rsi:
        c.wait_send()


def keep_both(a, b, c, d):
    c[...] = a[...]
    d[...] = b[...]


def local(user_emb, item_emb, user_deg, item_deg, tile_rows, tile_cols, tile_count, tiles):
    vmem = pl.BlockSpec(memory_space=pltpu.VMEM)
    smem = pl.BlockSpec(memory_space=pltpu.SMEM)
    dma = pltpu.SemaphoreType.DMA
    outs = (
        jax.ShapeDtypeStruct((SHARD, BLOCK), F32),
        jax.ShapeDtypeStruct((BLOCK, BLOCK), F32),
    )
    half_done = pl.pallas_call(
        layer,
        out_shape=outs,
        in_specs=[vmem] * 6 + [smem, pl.BlockSpec(memory_space=pl.ANY)],
        out_specs=(vmem, vmem),
        scratch_shapes=[
            pltpu.VMEM((SLOTS + 1, BLOCK, BLOCK), BF16),
            pltpu.VMEM((IBLOCKS, BLOCK, BLOCK), BF16),
            pltpu.VMEM((4, 8, SHARD, BLOCK), BF16),
            pltpu.VMEM((UBLOCKS, BLOCK, BLOCK), BF16),
            pltpu.VMEM((16, LANES), I32),
            pltpu.SMEM((16, LANES), I32),
            pltpu.VMEM((UPAIRS, BLOCK, BLOCK), F32),
            pltpu.VMEM((IPAIRS, BLOCK, BLOCK), F32),
            pltpu.VMEM((4, 8, SHARD, BLOCK), BF16),
            pltpu.VMEM((IBLOCKS, BLOCK, BLOCK), BF16),
            pltpu.VMEM((7, 4, SHARD, BLOCK), BF16),
            pltpu.VMEM((4, SHARD, BLOCK), F32),
            pltpu.VMEM((4, 4, SHARD, BLOCK), BF16),
            pltpu.VMEM((16, BLOCK, BLOCK), BF16),
            dma((2,)),
            dma((16,)), dma((16,)),
            dma((4,)), dma((4,)),
            dma((7,)), dma((7,)),
            dma((7,)), dma((7,)),
            dma((4,)), dma((4,)),
            dma((16,)), dma((16,)),
        ],
        compiler_params=pltpu.CompilerParams(
            collective_id=0, has_side_effects=True, vmem_limit_bytes=40 * 1024 * 1024
        ),
        name="layer",
    )(
        user_emb, item_emb, user_deg.reshape(UBLOCKS, BLOCK), item_deg.reshape(IBLOCKS, BLOCK),
        tile_rows, tile_cols, tile_count, tiles,
    )
    return pl.pallas_call(
        keep_both, out_shape=outs, in_specs=[vmem, vmem], out_specs=(vmem, vmem), name="keep"
    )(*half_done)


def solution(mesh):
    return jax.shard_map(
        local,
        mesh=mesh,
        in_specs=(
            P(("user", "item"), None),
            P(("item", "user"), None),
            P("user"),
            P("item"),
            P("user", "item", None),
            P("user", "item", None),
            P("user", "item"),
            P("user", "item", None, None, None),
        ),
        out_specs=(P(("user", "item"), None), P(("item", "user"), None)),
        check_vma=False,
    )
```

time: 926 us -> 59.3 us (0.06); the launches traced: 914 us -> 58.9 us
  waiting for transfers between devices: 723 us -> 0 us
  blocking collectives: 92.1 us -> 0 us
  Pallas kernels: 0 us -> 49.9 us
  other arithmetic: 42.8 us -> 0 us
  matrix products: 21.6 us -> 0 us
  between operations: 14.1 us -> 1.31 us
  local copies, waits for them, and re-layouts: 18.8 us -> 7.67 us
    reduce_scatter x2 -> x0, waiting for transfers between devices: 723 us -> none  [the longest x1 650 us: reduce_users(): lax.psum_scatter(user_total.reshape(-1, feature), 'item', scatter_dimensi...]
    all_gather x2 -> x0, blocking collectives: 92.1 us -> none  [the longest x1 71.5 us: fetch_users(): return lax.all_gather(user_src, 'item', axis=0, tiled=True)]
    pallas_call x0 -> x2, Pallas kernels: none -> 49.9 us  [the longest x1 48.4 us: local(): pl.pallas_call(layer, out_shape=outs, in_specs=[vmem] * 6 + [smem, pl.Blo...]
    scatter-add x16 -> x0, other arithmetic: 25.7 us -> none  [the longest x8 12.8 us: advance(): item_total.at[cols_now].add(product * alive_mask[:, None, None])]
    dot_general x16 -> x0, matrix products: 21.6 us -> none  [the longest x8 10.8 us: advance(): jnp.einsum('tij,tjd->tid', tile_group, chosen, preferred_element_type=jnp...]
    convert_element_type x17 -> x0, other arithmetic: 11.2 us -> none  [the longest x16 10.4 us: advance(): alive_mask = (slot_now < live_count).astype(jnp.float32)]
    gather x16 -> x0, local copies, waits for them, and re-layouts: 10.4 us -> none  [the longest x8 5.19 us: advance(): chosen = user_blocks[rows_now]]
  transfers between devices with their start and end apart: 2 -> 0, of which waited for: 2 -> 0; matrix products, arithmetic and copies ran while one was open for 0% -> 0% of each run, Pallas kernels for 0% -> 0%
where the time goes in v1:
time: 59.3 us; the launch traced here: 58.9 us
  Pallas kernels  49.9 us (84%)
  local copies, waits for them, and re-layouts  7.67 us (13%)
  between operations  1.31 us (2%)
    pallas_call x1, Pallas kernels, local(): pl.pallas_call(layer, out_shape=outs, in_specs=[vmem] * 6 + [smem, pl.Blo...  48.4 us
    unnamed x18, local copies, waits for them, and re-layouts  7.67 us
    pallas_call x1, Pallas kernels, local(): pl.pallas_call(keep_both, out_shape=outs, in_specs=[vmem, vmem], out_spec...  1.5 us

profile of v1, /device:TPU:1, one launch (start us, length us, event | category | flops | bytes accessed | tf_op | source)
XLA Modules:
  0.0 58.9 jit_solution(5010294463598098953)
XLA Ops:
  1.3 0.0 copy-start
  1.3 2.2 %copy-done = bf16[1,1,128,128,128]{4,3,2,1,0:T(8,128)(2,1)S(1)} copy-done((bf16[1,1,128,128,128]{4,3,2,1,0:T(8,128)(2,1)S(1)}, bf16[1,1,128,128,128]{4,3,2,1,0:T(8,128)(2,1)}, u32[]{:S(2)}) %copy-start) | copy-done | bytes 4194328
  3.5 0.0 copy-start.1
  3.5 0.8 %copy-done.1 = f32[128,128]{1,0:T(8,128)S(1)} copy-done((f32[128,128]{1,0:T(8,128)S(1)}, f32[128,128]{1,0:T(8,128)}, u32[]{:S(2)}) %copy-start.1) | copy-done | bytes 65560
  4.3 0.0 copy-start.3
  4.3 0.7 %copy-done.3 = f32[48,128]{1,0:T(8,128)S(1)} copy-done((f32[48,128]{1,0:T(8,128)S(1)}, f32[48,128]{1,0:T(8,128)}, u32[]{:S(2)}) %copy-start.3) | copy-done | bytes 24600
  5.0 0.0 copy-start.5
  5.0 0.7 %copy-done.5 = s32[1536]{0:T(1024)S(1)} copy-done((s32[1536]{0:T(1024)S(1)}, s32[1536]{0:T(1024)}, u32[]{:S(2)}) %copy-start.5) | copy-done | bytes 6168
  5.7 0.0 copy-start.6
  5.7 0.7 %copy-done.6 = s32[2048]{0:T(1024)S(1)} copy-done((s32[2048]{0:T(1024)S(1)}, s32[2048]{0:T(1024)}, u32[]{:S(2)}) %copy-start.6) | copy-done | bytes 8216
  6.4 0.0 copy-start.7
  6.4 0.7 %copy-done.7 = s32[1,1,128]{2,1,0:T(1,128)S(1)} copy-done((s32[1,1,128]{2,1,0:T(1,128)S(1)}, s32[1,1,128]{2,1,0:T(1,128)}, u32[]{:S(2)}) %copy-start.7) | copy-done | bytes 536
  7.1 0.0 copy-start.8
  7.1 0.7 %copy-done.8 = s32[1,1,128]{2,1,0:T(1,128)S(1)} copy-done((s32[1,1,128]{2,1,0:T(1,128)S(1)}, s32[1,1,128]{2,1,0:T(1,128)}, u32[]{:S(2)}) %copy-start.8) | copy-done | bytes 536
  7.8 48.4 %layer.1 = (f32[48,128]{1,0:T(8,128)S(1)}, f32[128,128]{1,0:T(8,128)S(1)}) custom-call(f32[48,128]{1,0:T(8,128)S(1)} %copy-done.3, f32[128,128]{1,0:T(8,128)S(1)} %copy-done.1, s32[12,128]{1,0:T(8,128)S(1)} %bitcast.2, s32[16,128]{1,0:T(8,128)S(1)} %bitcast.3, s32[1,1,128]{2,1,0:T(1,128)S(1)} %copy-done.7, s32[1,1,128]{2,1,0:T(1,128)S(1)} %copy-done.8, ...), custom_call_target="tpu_custom_call" | custom-call | tf_op jit(solution)/shard_map/layer/pallas_call | solution.py:272
  56.2 0.0 copy-start.2
  56.2 0.6 %copy-done.2 = f32[128,128]{1,0:T(8,128)} copy-done((f32[128,128]{1,0:T(8,128)}, f32[128,128]{1,0:T(8,128)S(1)}, u32[]{:S(2)}) %copy-start.2) | copy-done | bytes 65560
  56.8 0.0 copy-start.4
  56.8 0.6 %copy-done.4 = f32[48,128]{1,0:T(8,128)} copy-done((f32[48,128]{1,0:T(8,128)}, f32[48,128]{1,0:T(8,128)S(1)}, u32[]{:S(2)}) %copy-start.4) | copy-done | bytes 24600
  57.4 1.5 %keep.1 = (f32[48,128]{1,0:T(8,128)}, f32[128,128]{1,0:T(8,128)}) custom-call(f32[48,128]{1,0:T(8,128)} %copy-done.4, f32[128,128]{1,0:T(8,128)} %copy-done.2), custom_call_target="tpu_custom_call" | custom-call | tf_op jit(solution)/shard_map/keep/pallas_call | solution.py:308
Async XLA Ops:
  1.3 2.2 %copy-start = (bf16[1,1,128,128,128]{4,3,2,1,0:T(8,128)(2,1)S(1)}, bf16[1,1,128,128,128]{4,3,2,1,0:T(8,128)(2,1)}, u32[]{:S(2)}) copy-start(bf16[1,1,128,128,128]{4,3,2,1,0:T(8,128)(2,1)} %tiles_hbm.1) | copy-start | bytes 12582916
  3.5 0.8 %copy-start.1 = (f32[128,128]{1,0:T(8,128)S(1)}, f32[128,128]{1,0:T(8,128)}, u32[]{:S(2)}) copy-start(f32[128,128]{1,0:T(8,128)} %item_emb.1) | copy-start | bytes 196612
  4.3 0.7 %copy-start.3 = (f32[48,128]{1,0:T(8,128)S(1)}, f32[48,128]{1,0:T(8,128)}, u32[]{:S(2)}) copy-start(f32[48,128]{1,0:T(8,128)} %user_emb.1) | copy-start | bytes 73732
  5.0 0.7 %copy-start.5 = (s32[1536]{0:T(1024)S(1)}, s32[1536]{0:T(1024)}, u32[]{:S(2)}) copy-start(s32[1536]{0:T(1024)} %param.10) | copy-start | bytes 18436
  5.7 0.7 %copy-start.6 = (s32[2048]{0:T(1024)S(1)}, s32[2048]{0:T(1024)}, u32[]{:S(2)}) copy-start(s32[2048]{0:T(1024)} %param.11) | copy-start | bytes 24580
  6.4 0.7 %copy-start.7 = (s32[1,1,128]{2,1,0:T(1,128)S(1)}, s32[1,1,128]{2,1,0:T(1,128)}, u32[]{:S(2)}) copy-start(s32[1,1,128]{2,1,0:T(1,128)} %rows_ref.1) | copy-start | bytes 1540
  7.1 0.7 %copy-start.8 = (s32[1,1,128]{2,1,0:T(1,128)S(1)}, s32[1,1,128]{2,1,0:T(1,128)}, u32[]{:S(2)}) copy-start(s32[1,1,128]{2,1,0:T(1,128)} %cols_ref.1) | copy-start | bytes 1540
  56.2 0.6 %copy-start.2 = (f32[128,128]{1,0:T(8,128)}, f32[128,128]{1,0:T(8,128)S(1)}, u32[]{:S(2)}) copy-start(f32[128,128]{1,0:T(8,128)S(1)} %get-tuple-element.5.b) | copy-start | bytes 196612
  56.8 0.6 %copy-start.4 = (f32[48,128]{1,0:T(8,128)}, f32[48,128]{1,0:T(8,128)S(1)}, u32[]{:S(2)}) copy-start(f32[48,128]{1,0:T(8,128)S(1)} %get-tuple-element.4.a) | copy-start | bytes 73732

commit v2 on v1

v2 whole, which is shorter than its diff:
```python
import functools

import jax
import jax.numpy as jnp
from jax import lax
from jax.experimental import pallas as pl
from jax.experimental.pallas import tpu as pltpu
from jax.sharding import PartitionSpec as P

MESH = pl.DeviceIdType.MESH
F32, BF16, I32 = jnp.float32, jnp.bfloat16, jnp.int32

USERS_AXIS = 16
BLOCK = 128
SLOTS = 128
UBLOCKS, IBLOCKS = 12, 16
SHARD = 48
UPAIRS = (SLOTS + UBLOCKS) // 2
IPAIRS = (SLOTS + IBLOCKS) // 2
LANES = 256
UUNROLL, IUNROLL = 35, 24


def iota(shape, dim):
    return lax.broadcasted_iota(I32, shape, dim)


def count(mask, dim):
    return jnp.sum(jnp.where(mask, 1, 0).astype(I32), axis=dim, keepdims=True)


def column(lanes):
    eye = iota((SLOTS, SLOTS), 0) == iota((SLOTS, SLOTS), 1)
    return jnp.sum(jnp.where(eye, lanes, 0), axis=1, keepdims=True)


def order(keys, others, live):
    keys_c, others_c = column(keys), column(others)
    at_lane, at_row = iota((SLOTS, SLOTS), 1), iota((SLOTS, SLOTS), 0)
    alive_l = at_lane < live
    alive_c = iota((SLOTS, 1), 0) < live
    ahead = (keys_c == keys) & (at_lane < at_row) & alive_l
    rank_c = count(ahead, 1)
    hits_l = count((keys_c == at_lane) & (at_row < live), 0)
    hits_c = column(hits_l)
    padded_l = ((hits_l + 1) >> 1) << 1
    padded_c = ((hits_c + 1) >> 1) << 1
    base_l = jnp.sum(jnp.where(at_row < at_lane, padded_c, 0), axis=0, keepdims=True)
    base_c = jnp.sum(jnp.where(at_lane < at_row, padded_l, 0), axis=1, keepdims=True)
    place_c = jnp.sum(jnp.where(at_lane < keys_c, padded_l, 0), axis=1, keepdims=True) + rank_c
    places = iota((SLOTS, LANES), 1)
    slots = iota((SLOTS, LANES), 0)
    mine = (place_c == places) & alive_c
    slot = jnp.sum(jnp.where(mine, slots + 1, 0), axis=0, keepdims=True)
    slot = jnp.where(slot == 0, SLOTS, slot - 1)
    other = jnp.sum(jnp.where(mine, others_c, 0), axis=0, keepdims=True)
    opens = (base_c == places) & (hits_c > 0)
    keep = 1 - jnp.minimum(count(opens, 0), 1)
    last = ((base_l + padded_l) >> 1) - 1
    last = jnp.maximum(last, 0)
    some = jnp.minimum(hits_l, 1)
    return slot, other, keep, last, some


def own_scale(deg_ref, first, rows):
    blocks = deg_ref.shape[0]
    out = jnp.zeros((rows, 1), I32)
    for b in range(blocks):
        here = iota((rows, BLOCK), 1) + b * BLOCK == iota((rows, BLOCK), 0) + first
        out = out + jnp.sum(jnp.where(here, deg_ref[b : b + 1, :], 0), axis=1, keepdims=True)
    return lax.rsqrt(out.astype(F32))


def layer(
    user_emb_h, item_emb_h, user_deg_h, item_deg_h, rows_h, cols_h, live_h, tiles_h,
    user_out, item_out,
    user_emb, item_emb, user_deg, item_deg, rows_v, cols_v, live_v,
    tiles, item_src, users, user_src_t, meta_v, meta, run_u, run_i, part_u, part_i,
    got1, keep1, send2, got2, got_i,
    local_sem, ag_a_s, ag_a_r, ag_b_s, ag_b_r, ag_i_s, ag_i_r, ag_f_s, ag_f_r,
    rs1_s, rs1_r, rs2_s, rs2_r, rsi_s, rsi_r,
):
    u, i = lax.axis_index("user"), lax.axis_index("item")
    z, xh = i // 2, lax.rem(i, 2)
    zh, zl = z // 4, lax.rem(z, 4)
    kind = 2 * zl + xh
    twin = u + 1 - 2 * lax.rem(u, 2)

    def plane(dz):
        return lax.rem(z + dz + 16, 16)

    def at(dz, other):
        return {"item": 2 * plane(dz) + (1 - xh if other else xh)}

    def send(src, dst, sems, where, there):
        return pltpu.make_async_remote_copy(
            src_ref=src, dst_ref=dst, send_sem=sems[0].at[where[0]], recv_sem=sems[1].at[where[1]],
            device_id=there, device_id_type=MESH)

    ins = [
        pltpu.make_async_copy(a, b, local_sem.at[n]) for n, (a, b) in enumerate((
            (item_deg_h, item_deg), (item_emb_h, item_emb), (user_deg_h, user_deg), (user_emb_h, user_emb),
            (rows_h, rows_v), (cols_h, cols_v), (live_h, live_v), (tiles_h.at[0, 0], tiles.at[pl.ds(0, SLOTS)])))
    ]
    for c in ins:
        c.start()

    barrier = pltpu.get_barrier_semaphore()
    near = [(dz, o) for dz in (-2, -1, 0, 1, 2) for o in (False, True) if dz or o]
    far = [(8, False), (4, False), (12, False)]
    for dz, o in far + near:
        pl.semaphore_signal(barrier, inc=1, device_id=at(dz, o), device_id_type=MESH)
    for k in range(1, 8):
        pl.semaphore_signal(barrier, inc=1, device_id={"user": lax.rem(u + 2 * k, 16)}, device_id_type=MESH)
    pl.semaphore_signal(barrier, inc=1, device_id={"user": twin}, device_id_type=MESH)
    for k in range(1, 8):
        pl.semaphore_signal(barrier, inc=1, device_id={"user": lax.rem(twin + 2 * k, 16)}, device_id_type=MESH)

    for n in range(4):
        ins[n].wait()
    scale_i = own_scale(item_deg, u * BLOCK, BLOCK)
    item_src[u] = (item_emb[...] * scale_i).astype(BF16)
    scale_u = own_scale(user_deg, i * SHARD, SHARD)
    users[zh, kind] = (user_emb[...] * scale_u).astype(BF16)
    pl.semaphore_wait(barrier, 15 + len(near) + len(far))

    ag_a = [
        send(users.at[zh, kind], users.at[zh, kind], (ag_a_s, ag_a_r), (k, k), at(4 * k, False)) for k in (2, 1, 3)
    ]
    for c in ag_a:
        c.start()
    ag_i = [
        send(item_src.at[u], item_src.at[u], (ag_i_s, ag_i_r), (k, k), {"user": lax.rem(u + 2 * k, 16)})
        for k in range(1, 8)
    ]
    for c in ag_i:
        c.start()
    ag_f = [send(item_src.at[u], item_src.at[u], (ag_f_s, ag_f_r), (0, 0), {"user": twin})]
    ag_f[0].start()

    turn = 2 * plane(2) * (1 - xh) + 2 * plane(-2) * xh
    ag_b = []

    def spread(h):
        row = users.at[h, kind]
        for dz, o in ((0, True), (1, False), (1, True), (-1, False), (-1, True)):
            ag_b.append(send(row, row, (ag_b_s, ag_b_r), (0, 0), at(dz, o)))
        for half in range(2):
            ag_b.append(send(row, row, (ag_b_s, ag_b_r), (0, 0), {"item": turn + half}))
        for c in ag_b[-7:]:
            c.start()

    spread(zh)

    for n in range(4, 7):
        ins[n].wait()
    rows, cols, live = rows_v[0], cols_v[0], live_v[...]
    parts = order(rows, cols, live) + order(cols, rows, live)
    meta_v[...] = jnp.zeros_like(meta_v)
    for n, part in enumerate(parts):
        meta_v[n : n + 1, 0 : part.shape[1]] = part
    to_scalar = pltpu.make_async_copy(meta_v, meta, local_sem.at[8])
    to_scalar.start()
    tiles[SLOTS] = jnp.zeros((BLOCK, BLOCK), BF16)

    for k in range(1, 8):
        ag_i[k - 1].wait_recv()
        came = lax.rem(u - 2 * k + 16, 16)
        c = send(item_src.at[came], item_src.at[came], (ag_f_s, ag_f_r), (0, 0), {"user": twin})
        c.start()
        ag_f.append(c)
    for n, k in ((1, 1), (2, 3), (0, 2)):
        ag_a[n].wait_recv()
        spread(lax.rem(zh - k + 4, 4))

    to_scalar.wait()
    ins[7].wait()
    send(item_src.at[0:8], item_src.at[0:8], (ag_f_s, ag_f_r), (0, 0), {"user": twin}).wait_recv()

    def user_step(q, acc):
        s0, s1 = meta[0, 2 * q], meta[0, 2 * q + 1]
        c0, c1 = meta[1, 2 * q], meta[1, 2 * q + 1]
        keep = meta[2, 2 * q].astype(F32)
        left = jnp.concatenate([tiles[s0], tiles[s1]], axis=1)
        right = jnp.concatenate([item_src[c0], item_src[c1]], axis=0)
        acc = acc * keep + jnp.dot(left, right, preferred_element_type=F32)
        run_u[q] = acc
        return acc

    lax.fori_loop(0, UPAIRS, user_step, jnp.zeros((BLOCK, BLOCK), F32), unroll=UUNROLL)
    for r in range(UBLOCKS):
        total = (run_u[meta[3, r]] * meta[4, r].astype(F32)).astype(BF16)
        for j in range(8):
            g = 8 * r + j
            part_u[g // 24, (g % 24) // 3, 16 * (g % 3) : 16 * (g % 3) + 16, :] = total[16 * j : 16 * j + 16]

    rs1 = []
    for k in (2, 1, 3, 0):
        for n, (dz, o) in enumerate(((0, True), (1, False), (1, True), (-1, False), (-1, True))):
            there = 2 * lax.rem(zl + dz + 4, 4) + (1 - xh if o else xh)
            rs1.append(send(part_u.at[lax.rem(plane(dz) // 4 + k, 4), there], got1.at[k, n], (rs1_s, rs1_r), (0, k), at(dz, o)))
        for half in range(2):
            there = 2 * lax.rem(zl + 2, 4) + half
            dz = 2 - 4 * half
            rs1.append(send(part_u.at[lax.rem(plane(dz) // 4 + k, 4), there], got1.at[k, 5 + xh], (rs1_s, rs1_r), (0, k),
                            {"item": 2 * plane(dz) + half}))
        for c in rs1[-7:]:
            c.start()

    send(users.at[:, 0:7], users.at[:, 0:7], (ag_b_s, ag_b_r), (0, 0), at(1, False)).wait_recv()
    for r in range(UBLOCKS):
        groups = []
        for j in range(8):
            g = 8 * r + j
            groups.append(users[g // 24, (g % 24) // 3, 16 * (g % 3) : 16 * (g % 3) + 16, :])
        user_src_t[r] = jnp.concatenate(groups, axis=0).T

    def item_step(q, acc):
        s0, s1 = meta[5, 2 * q], meta[5, 2 * q + 1]
        r0, r1 = meta[6, 2 * q], meta[6, 2 * q + 1]
        keep = meta[7, 2 * q].astype(F32)
        left = jnp.concatenate([user_src_t[r0], user_src_t[r1]], axis=1)
        right = jnp.concatenate([tiles[s0], tiles[s1]], axis=0)
        acc = acc * keep + jnp.dot(left, right, preferred_element_type=F32)
        run_i[q] = acc
        return acc

    lax.fori_loop(0, IPAIRS, item_step, jnp.zeros((BLOCK, BLOCK), F32), unroll=IUNROLL)
    for c in range(IBLOCKS):
        part_i[c] = (run_i[meta[8, c]] * meta[9, c].astype(F32)).astype(BF16)
    rsi = []
    for k in range(1, 16):
        there = lax.rem(u + k, 16)
        rsi.append(send(part_i.at[there], got_i.at[k], (rsi_s, rsi_r), (0, 0), {"user": there}))
    for c in rsi:
        c.start()

    rs2 = []
    for k in (2, 1, 3, 0):
        send(got1.at[k], got1.at[k], (rs1_s, rs1_r), (0, k), at(1, False)).wait_recv()
        total = part_u[lax.rem(zh + k, 4), kind].astype(F32)
        for n in range(7):
            total = total + got1[k, n].astype(F32)
        if k:
            send2[k] = total.astype(BF16)
            rs2.append(send(send2.at[k], got2.at[k], (rs2_s, rs2_r), (0, 0), at(4 * k, False)))
            rs2[-1].start()
        else:
            keep1[...] = total

    send(got_i.at[1:16], got_i.at[1:16], (rsi_s, rsi_r), (0, 0), {"user": twin}).wait_recv()
    total = part_i[u].astype(F32)
    for k in range(1, 16):
        total = total + got_i[k].astype(F32)
    item_out[...] = total.T * scale_i

    send(got2.at[1:4], got2.at[1:4], (rs2_s, rs2_r), (0, 0), at(1, False)).wait_recv()
    total = keep1[...]
    for k in range(1, 4):
        total = total + got2[k].astype(F32)
    user_out[...] = total * scale_u

    for c in ag_a + ag_i:
        c.wait_send()
    send(item_src.at[0:8], item_src.at[0:8], (ag_f_s, ag_f_r), (0, 0), {"user": twin}).wait_send()
    send(users.at[:, 0:7], users.at[:, 0:7], (ag_b_s, ag_b_r), (0, 0), at(1, False)).wait_send()
    send(part_u.at[:, 0:7], part_u.at[:, 0:7], (rs1_s, rs1_r), (0, 0), at(1, False)).wait_send()
    send(got_i.at[1:16], got_i.at[1:16], (rsi_s, rsi_r), (0, 0), {"user": twin}).wait_send()
    send(got2.at[1:4], got2.at[1:4], (rs2_s, rs2_r), (0, 0), at(1, False)).wait_send()


def hand_over(a, b, c, d, sem):
    copies = [pltpu.make_async_copy(a, c, sem.at[0]), pltpu.make_async_copy(b, d, sem.at[1])]
    for copy in copies:
        copy.start()
    for copy in copies:
        copy.wait()


def local(user_emb, item_emb, user_deg, item_deg, tile_rows, tile_cols, tile_count, tiles):
    hbm = pl.BlockSpec(memory_space=pltpu.HBM)
    dma = pltpu.SemaphoreType.DMA
    outs = (jax.ShapeDtypeStruct((SHARD, BLOCK), F32), jax.ShapeDtypeStruct((BLOCK, BLOCK), F32))
    vmem = pl.BlockSpec(memory_space=pltpu.VMEM)
    sums = pl.pallas_call(
        layer,
        out_shape=(pltpu.VMEM((SHARD, BLOCK), F32), pltpu.VMEM((BLOCK, BLOCK), F32)),
        in_specs=[hbm] * 8,
        out_specs=(vmem, vmem),
        scratch_shapes=[
            pltpu.VMEM((SHARD, BLOCK), F32),
            pltpu.VMEM((BLOCK, BLOCK), F32),
            pltpu.VMEM((UBLOCKS, BLOCK), I32),
            pltpu.VMEM((IBLOCKS, BLOCK), I32),
            pltpu.VMEM((1, 1, SLOTS), I32),
            pltpu.VMEM((1, 1, SLOTS), I32),
            pltpu.VMEM((1, 1), I32),
            pltpu.VMEM((SLOTS + 1, BLOCK, BLOCK), BF16),
            pltpu.VMEM((IBLOCKS, BLOCK, BLOCK), BF16),
            pltpu.VMEM((4, 8, SHARD, BLOCK), BF16),
            pltpu.VMEM((UBLOCKS, BLOCK, BLOCK), BF16),
            pltpu.VMEM((16, LANES), I32),
            pltpu.SMEM((16, LANES), I32),
            pltpu.VMEM((UPAIRS, BLOCK, BLOCK), F32),
            pltpu.VMEM((IPAIRS, BLOCK, BLOCK), F32),
            pltpu.VMEM((4, 8, SHARD, BLOCK), BF16),
            pltpu.VMEM((IBLOCKS, BLOCK, BLOCK), BF16),
            pltpu.VMEM((4, 7, SHARD, BLOCK), BF16),
            pltpu.VMEM((SHARD, BLOCK), F32),
            pltpu.VMEM((4, SHARD, BLOCK), BF16),
            pltpu.VMEM((4, SHARD, BLOCK), BF16),
            pltpu.VMEM((16, BLOCK, BLOCK), BF16),
            dma((11,)),
            dma((4,)), dma((4,)),
            dma((1,)), dma((1,)),
            dma((8,)), dma((8,)),
            dma((1,)), dma((1,)),
            dma((1,)), dma((4,)),
            dma((1,)), dma((1,)),
            dma((1,)), dma((1,)),
        ],
        compiler_params=pltpu.CompilerParams(
            collective_id=0, has_side_effects=True, vmem_limit_bytes=60 * 1024 * 1024
        ),
        name="layer",
    )(
        user_emb, item_emb, user_deg.reshape(UBLOCKS, BLOCK), item_deg.reshape(IBLOCKS, BLOCK),
        tile_rows, tile_cols, tile_count, tiles,
    )
    return pl.pallas_call(
        hand_over,
        out_shape=outs,
        in_specs=[vmem, vmem],
        out_specs=(hbm, hbm),
        scratch_shapes=[dma((2,))],
        compiler_params=pltpu.CompilerParams(vmem_limit_bytes=16 * 1024 * 1024),
        name="hand_over",
    )(*sums)


def solution(mesh):
    return jax.shard_map(
        local,
        mesh=mesh,
        in_specs=(
            P(("user", "item"), None),
            P(("item", "user"), None),
            P("user"),
            P("item"),
            P("user", "item", None),
            P("user", "item", None),
            P("user", "item"),
            P("user", "item", None, None, None),
        ),
        out_specs=(P(("user", "item"), None), P(("item", "user"), None)),
        check_vma=False,
    )
```

time: 59.3 us -> 41.4 us (0.70)
  Pallas kernels: 49.9 us -> 39.9 us
  local copies, waits for them, and re-layouts: 7.67 us -> 0 us
    pallas_call x2, Pallas kernels: 49.9 us -> 39.9 us  [the longest x1 39.3 us: local(): pl.pallas_call(layer, out_shape=(pltpu.VMEM((SHARD, BLOCK), F32), pltpu.V...]
    unnamed x18 -> x0, local copies, waits for them, and re-layouts: 7.67 us -> none
where the time goes in v2:
time: 41.4 us; the launch traced here: 41.2 us
  Pallas kernels  39.9 us (96%)
  between operations  1.29 us (3%)
    pallas_call x1, Pallas kernels, local(): pl.pallas_call(layer, out_shape=(pltpu.VMEM((SHARD, BLOCK), F32), pltpu.V...  39.3 us

profile of v2, /device:TPU:1, one launch (start us, length us, event | category | flops | bytes accessed | tf_op | source)
XLA Modules:
  0.0 41.2 jit_solution(9696730756639133709)
XLA Ops:
  1.3 39.3 %layer.1 = (f32[48,128]{1,0:T(8,128)S(1)}, f32[128,128]{1,0:T(8,128)S(1)}) custom-call(f32[48,128]{1,0:T(8,128)} %user_emb_h.1, f32[128,128]{1,0:T(8,128)} %item_emb_h.1, s32[12,128]{1,0:T(8,128)} %bitcast.2, s32[16,128]{1,0:T(8,128)} %bitcast.3, s32[1,1,128]{2,1,0:T(1,128)} %rows_h.1, s32[1,1,128]{2,1,0:T(1,128)} %cols_h.1, s32[1,1]{1,0:T(1,128)S(6)} %copy.10.live_h, ...), custom_call_target="tpu_custom_call" | custom-call | tf_op jit(solution)/shard_map/layer/pallas_call | solution.py:285
  40.5 0.7 %hand_over.1 = (f32[48,128]{1,0:T(8,128)}, f32[128,128]{1,0:T(8,128)}) custom-call(f32[48,128]{1,0:T(8,128)S(1)} %get-tuple-element.4.a, f32[128,128]{1,0:T(8,128)S(1)} %get-tuple-element.5.b), custom_call_target="tpu_custom_call" | custom-call | tf_op jit(solution)/shard_map/hand_over/pallas_call | solution.py:330

commit v3 on v2

--- a/solution.py
+++ b/solution.py
@@ -18,7 +18,7 @@
 UPAIRS = (SLOTS + UBLOCKS) // 2
 IPAIRS = (SLOTS + IBLOCKS) // 2
 LANES = 256
-UUNROLL, IUNROLL = 35, 24
+UUNROLL, IUNROLL = 70, 72
 
 
 def iota(shape, dim):
@@ -150,7 +150,6 @@
         for c in ag_b[-7:]:
             c.start()
 
-    spread(zh)
 
     for n in range(4, 7):
         ins[n].wait()
@@ -162,6 +161,8 @@
     to_scalar = pltpu.make_async_copy(meta_v, meta, local_sem.at[8])
     to_scalar.start()
     tiles[SLOTS] = jnp.zeros((BLOCK, BLOCK), BF16)
+
+    spread(zh)
 
     for k in range(1, 8):
         ag_i[k - 1].wait_recv()

time: 41.4 us -> 40.7 us (0.983)
  Pallas kernels: 39.9 us -> 39.3 us
    pallas_call x1, Pallas kernels: 39.3 us -> 38.6 us  [local(): pl.pallas_call(layer, out_shape=(pltpu.VMEM((SHARD, BLOCK), F32), pltpu.V...]
where the time goes in v3:
time: 40.7 us; the launch traced here: 40.5 us
  Pallas kernels  39.3 us (97%)
  between operations  1.29 us (3%)
    pallas_call x1, Pallas kernels, local(): pl.pallas_call(layer, out_shape=(pltpu.VMEM((SHARD, BLOCK), F32), pltpu.V...  38.6 us

profile of v3, /device:TPU:1, one launch (start us, length us, event | category | flops | bytes accessed | tf_op | source)
XLA Modules:
  0.0 40.5 jit_solution(4506000361052546992)
XLA Ops:
  1.3 38.6 %layer.1 = (f32[48,128]{1,0:T(8,128)S(1)}, f32[128,128]{1,0:T(8,128)S(1)}) custom-call(f32[48,128]{1,0:T(8,128)} %user_emb_h.1, f32[128,128]{1,0:T(8,128)} %item_emb_h.1, s32[12,128]{1,0:T(8,128)} %bitcast.2, s32[16,128]{1,0:T(8,128)} %bitcast.3, s32[1,1,128]{2,1,0:T(1,128)} %rows_h.1, s32[1,1,128]{2,1,0:T(1,128)} %cols_h.1, s32[1,1]{1,0:T(1,128)S(6)} %copy.10.live_h, ...), custom_call_target="tpu_custom_call" | custom-call | tf_op jit(solution)/shard_map/layer/pallas_call | solution.py:286
  39.9 0.7 %hand_over.1 = (f32[48,128]{1,0:T(8,128)}, f32[128,128]{1,0:T(8,128)}) custom-call(f32[48,128]{1,0:T(8,128)S(1)} %get-tuple-element.4.a, f32[128,128]{1,0:T(8,128)S(1)} %get-tuple-element.5.b), custom_call_target="tpu_custom_call" | custom-call | tf_op jit(solution)/shard_map/hand_over/pallas_call | solution.py:331

commit v4 on v3

--- a/solution.py
+++ b/solution.py
@@ -170,9 +170,12 @@
         c = send(item_src.at[came], item_src.at[came], (ag_f_s, ag_f_r), (0, 0), {"user": twin})
         c.start()
         ag_f.append(c)
-    for n, k in ((1, 1), (2, 3), (0, 2)):
-        ag_a[n].wait_recv()
-        spread(lax.rem(zh - k + 4, 4))
+        if k in (4, 6):
+            n = k // 2 - 1
+            ag_a[n].wait_recv()
+            spread(lax.rem(zh + (2 * n + 1), 4))
+    ag_a[0].wait_recv()
+    spread(lax.rem(zh + 2, 4))
 
     to_scalar.wait()
     ins[7].wait()
@@ -230,7 +233,7 @@
     for c in range(IBLOCKS):
         part_i[c] = (run_i[meta[8, c]] * meta[9, c].astype(F32)).astype(BF16)
     rsi = []
-    for k in range(1, 16):
+    for k in (12, 13, 4, 5, 11, 10, 14, 15, 6, 7, 3, 2, 9, 8, 1):
         there = lax.rem(u + k, 16)
         rsi.append(send(part_i.at[there], got_i.at[k], (rsi_s, rsi_r), (0, 0), {"user": there}))
     for c in rsi:

time: 40.7 us -> 40.3 us (level)
  Pallas kernels: 39.3 us -> 38.8 us
    pallas_call x1, Pallas kernels: 38.6 us -> 38.2 us  [local(): pl.pallas_call(layer, out_shape=(pltpu.VMEM((SHARD, BLOCK), F32), pltpu.V...]
where the time goes in v4:
time: 40.3 us; the launch traced here: 40.1 us
  Pallas kernels  38.8 us (96%)
  between operations  1.29 us (3%)
    pallas_call x1, Pallas kernels, local(): pl.pallas_call(layer, out_shape=(pltpu.VMEM((SHARD, BLOCK), F32), pltpu.V...  38.2 us

profile of v4, /device:TPU:1, one launch (start us, length us, event | category | flops | bytes accessed | tf_op | source)
XLA Modules:
  0.0 40.1 jit_solution(10347715699687795393)
XLA Ops:
  1.3 38.2 %layer.1 = (f32[48,128]{1,0:T(8,128)S(1)}, f32[128,128]{1,0:T(8,128)S(1)}) custom-call(f32[48,128]{1,0:T(8,128)} %user_emb_h.1, f32[128,128]{1,0:T(8,128)} %item_emb_h.1, s32[12,128]{1,0:T(8,128)} %bitcast.2, s32[16,128]{1,0:T(8,128)} %bitcast.3, s32[1,1,128]{2,1,0:T(1,128)} %rows_h.1, s32[1,1,128]{2,1,0:T(1,128)} %cols_h.1, s32[1,1]{1,0:T(1,128)S(6)} %copy.10.live_h, ...), custom_call_target="tpu_custom_call" | custom-call | tf_op jit(solution)/shard_map/layer/pallas_call | solution.py:289
  39.4 0.7 %hand_over.1 = (f32[48,128]{1,0:T(8,128)}, f32[128,128]{1,0:T(8,128)}) custom-call(f32[48,128]{1,0:T(8,128)S(1)} %get-tuple-element.4.a, f32[128,128]{1,0:T(8,128)S(1)} %get-tuple-element.5.b), custom_call_target="tpu_custom_call" | custom-call | tf_op jit(solution)/shard_map/hand_over/pallas_call | solution.py:334
